TPU v7x, 32 devices: a whole 2x2x4 slice. The times are simulated.
32 devices in a mesh: dp: 16 (over z, y, x), tensor: 2 (over core).
Axes of the slice: x: 2, y: 2, z: 4, core: 2. Of those that a mesh axis runs over, the one named last changes fastest.
Arguments:
- inputs: bfloat16 [16384, 1024], P('dp'), may hold values from -6 to 6
- cotangent: bfloat16 [16384, 1024], P('dp'), may hold values from -6 to 6
- segment_ids: int32 [16384], P('dp'), may hold values from 0 to 127, never falling along the last dimension, each value on 1 to 512 neighbouring positions
- attn_gain: float32 [1024], replicated, may hold values from 0.25 to 1.75
- w_query: bfloat16 [1024, 1024], P(None, 'tensor'), may hold values from -0.1875 to 0.1875
- w_key: bfloat16 [1024, 512], P(None, 'tensor'), may hold values from -0.1875 to 0.1875
- w_value: bfloat16 [1024, 512], P(None, 'tensor'), may hold values from -0.1875 to 0.1875
- query_gain: float32 [64], replicated, may hold values from 0.25 to 1.75
- key_gain: float32 [64], replicated, may hold values from 0.25 to 1.75
- w_output: bfloat16 [1024, 1024], P(None, 'tensor'), may hold values from -0.5 to 0.5
- ffn_gain: float32 [1024], replicated, may hold values from 0.25 to 1.75
- w_gate: bfloat16 [1024, 4608], P(None, 'tensor'), may hold values from -0.1875 to 0.1875
- w_up: bfloat16 [1024, 4608], P(None, 'tensor'), may hold values from -0.1875 to 0.1875
- w_down: bfloat16 [1024, 4608], P(None, 'tensor'), may hold values from -0.09375 to 0.09375
Outputs:
- block_out: bfloat16 [16384, 1024], P('dp')
- grad_inputs: bfloat16 [16384, 1024], P('dp')
- grad_attn_gain: float32 [1024], P('dp')
- grad_w_query: float32 [1024, 1024], P('dp', 'tensor')
- grad_w_key: float32 [1024, 512], P('dp', 'tensor')
- grad_w_value: float32 [1024, 512], P('dp', 'tensor')
- grad_query_gain: float32 [64], replicated
- grad_key_gain: float32 [64], replicated
- grad_w_output: float32 [1024, 1024], P('dp', 'tensor')
- grad_ffn_gain: float32 [1024], P('dp')
- grad_w_gate: float32 [1024, 4608], P('dp', 'tensor')
- grad_w_up: float32 [1024, 4608], P('dp', 'tensor')
- grad_w_down: float32 [1024, 4608], P('dp', 'tensor')
Inputs may be any that keep to these rules, and one draw needn't show every extreme that they name: `segment_ids`: ids never fall along the tokens; each document has 1 to 512 tokens, one of them exactly 512.
All inputs are finite; a program needn't handle non-finite values.
Results may differ from a plain program's by a relative error of at most 0.014.
The roundings to bfloat16 on the way count: a program that leaves them out, or rounds other values in their place, can miss the bound.
Values sent between devices are 32-bit elements; how exact they have to be, the bound alone decides.
No kernel may reach another device: no remote copies, remote signals or barrier semaphores. Data moves between devices by JAX's collectives and lax.ppermute only.
A program may use at most 192 MiB of HBM per device.

v0:
```python
import jax
import jax.numpy as jnp
from jax import lax
from jax.sharding import PartitionSpec as P

HEAD_DIM = 64


epsilon = 1e-05
rope_base = 1000000.0
masked_score = -1e30


def rms_scale(values, scales):
    return values * lax.rsqrt(jnp.mean(values * values, axis=-1, keepdims=True) + epsilon) * scales


def rope_tables(segments):
    length = segments.shape[0]
    places = jnp.arange(length, dtype=jnp.int32)
    earlier = jnp.concatenate([segments[:1] - 1, segments[:-1]])
    starts = lax.cummax(jnp.where(segments != earlier, places, 0), axis=0)
    offsets = (places - starts).astype(jnp.float32)
    halves = HEAD_DIM // 2
    inverse = rope_base ** (-2.0 * jnp.arange(halves, dtype=jnp.float32) / HEAD_DIM)
    angles = offsets[:, None] * inverse[None, :]
    return (jnp.cos(angles), jnp.sin(angles))


def rotate(values, cosine, sine):
    halves = HEAD_DIM // 2
    first = values[..., :halves]
    second = values[..., halves:]
    cos_wide = cosine[:, None, :]
    sin_wide = sine[:, None, :]
    return jnp.concatenate(
        [first * cos_wide - second * sin_wide, second * cos_wide + first * sin_wide], axis=-1
    )


def head_piece(linear, scales, cosine, sine):
    row_count = linear.shape[0]
    head_count = linear.shape[1] // HEAD_DIM
    shaped = linear.reshape(row_count, head_count, HEAD_DIM)
    return rotate(rms_scale(shaped, scales), cosine, sine).reshape(row_count, head_count * HEAD_DIM)


def matmul(left, right):
    return jnp.dot(left, right, preferred_element_type=jnp.float32)


def matmul_bt(left, right):
    return lax.dot_general(
        left, right, (((1,), (1,)), ((), ())), preferred_element_type=jnp.float32
    )


def matmul_at(left, right):
    return lax.dot_general(
        left, right, (((0,), (0,)), ((), ())), preferred_element_type=jnp.float32
    )


def per_device(
    inputs,
    cotangent,
    segment_ids,
    attn_gain,
    w_query,
    w_key,
    w_value,
    query_gain,
    key_gain,
    w_output,
    ffn_gain,
    w_gate,
    w_up,
    w_down,
):
    seq_len = inputs.shape[0]
    span = min(512, seq_len)
    count = seq_len // span
    scale = HEAD_DIM ** (-0.5)
    head_count = w_query.shape[1] // HEAD_DIM
    kv_count = w_key.shape[1] // HEAD_DIM
    groups = head_count // kv_count
    input_full = inputs.astype(jnp.float32)
    normed, norm_back = jax.vjp(rms_scale, input_full, attn_gain)
    normed_b = normed.astype(jnp.bfloat16)
    query_lin = matmul(normed_b, w_query)
    key_lin = matmul(normed_b, w_key)
    value_lin = matmul(normed_b, w_value)
    cosine, sine = rope_tables(segment_ids)
    query_rot, query_back = jax.vjp(
        lambda linear, scales: head_piece(linear, scales, cosine, sine), query_lin, query_gain
    )
    key_rot, key_back = jax.vjp(
        lambda linear, scales: head_piece(linear, scales, cosine, sine), key_lin, key_gain
    )
    q_four = query_rot.astype(jnp.bfloat16).reshape(seq_len, kv_count, groups, HEAD_DIM)
    k_three = key_rot.astype(jnp.bfloat16).reshape(seq_len, kv_count, HEAD_DIM)
    v_three = value_lin.astype(jnp.bfloat16).reshape(seq_len, kv_count, HEAD_DIM)

    def scores_of(offset, finish):
        raw = (
            jnp.einsum(
                "qkgd,skd->kgqs",
                q_four[offset:finish],
                k_three[:finish],
                preferred_element_type=jnp.float32,
            )
            * scale
        )
        row_ids = offset + jnp.arange(finish - offset, dtype=jnp.int32)
        col_ids = jnp.arange(finish, dtype=jnp.int32)
        allowed = (segment_ids[offset:finish, None] == segment_ids[None, :finish]) & (
            col_ids[None, :] <= row_ids[:, None]
        )
        return jnp.where(allowed, raw, masked_score)

    pieces = []
    log_sums = []
    for number in range(count):
        offset = number * span
        finish = offset + span
        scores = scores_of(offset, finish)
        row_max = jnp.max(scores, axis=-1, keepdims=True)
        powers = jnp.exp(scores - row_max)
        totals = jnp.sum(powers, axis=-1, keepdims=True)
        probs = powers / totals
        log_sums.append(row_max + jnp.log(totals))
        mixed_part = jnp.einsum(
            "kgqs,skd->qkgd",
            probs.astype(jnp.bfloat16),
            v_three[:finish],
            preferred_element_type=jnp.float32,
        )
        pieces.append(mixed_part.reshape(span, head_count * HEAD_DIM))
    mixed_b = jnp.concatenate(pieces, axis=0).astype(jnp.bfloat16)
    attn_out = lax.psum(matmul_bt(mixed_b, w_output), "tensor")
    middle = input_full + attn_out
    normed_two, norm_two_back = jax.vjp(rms_scale, middle, ffn_gain)
    normed_two_b = normed_two.astype(jnp.bfloat16)
    gate = matmul(normed_two_b, w_gate)
    upper = matmul(normed_two_b, w_up)
    hidden, swish_back = jax.vjp(lambda left, right: jax.nn.silu(left) * right, gate, upper)
    hidden_b = hidden.astype(jnp.bfloat16)
    ffn_out = lax.psum(matmul_bt(hidden_b, w_down), "tensor")
    block_out = (middle + ffn_out).astype(jnp.bfloat16)
    grad_w_down = matmul_at(cotangent, hidden_b)
    grad_hidden = matmul(cotangent, w_down)
    grad_gate, grad_upper = swish_back(grad_hidden)
    grad_gate_b = grad_gate.astype(jnp.bfloat16)
    grad_upper_b = grad_upper.astype(jnp.bfloat16)
    grad_w_gate = matmul_at(normed_two_b, grad_gate_b)
    grad_w_up = matmul_at(normed_two_b, grad_upper_b)
    grad_normed_two = lax.psum(
        matmul_bt(grad_gate_b, w_gate) + matmul_bt(grad_upper_b, w_up), "tensor"
    )
    grad_from_two, grad_ffn_gain = norm_two_back(grad_normed_two)
    grad_middle = cotangent.astype(jnp.float32) + grad_from_two
    grad_branch = grad_middle.astype(jnp.bfloat16)
    grad_w_output = matmul_at(grad_branch, mixed_b)
    grad_mixed = matmul(grad_branch, w_output).astype(jnp.bfloat16)
    grad_four = grad_mixed.reshape(seq_len, kv_count, groups, HEAD_DIM)
    query_grads = []
    grad_keys = jnp.zeros((seq_len, kv_count, HEAD_DIM), jnp.float32)
    grad_values = jnp.zeros((seq_len, kv_count, HEAD_DIM), jnp.float32)
    for number in range(count):
        offset = number * span
        finish = offset + span
        scores = scores_of(offset, finish)
        probs = jnp.exp(scores - log_sums[number])
        grad_block = grad_four[offset:finish]
        grad_probs = jnp.einsum(
            "qkgd,skd->kgqs", grad_block, v_three[:finish], preferred_element_type=jnp.float32
        )
        center = jnp.sum(grad_probs * probs, axis=-1, keepdims=True)
        grad_scores = (probs * (grad_probs - center)).astype(jnp.bfloat16)
        query_part = (
            jnp.einsum(
                "kgqs,skd->qkgd", grad_scores, k_three[:finish], preferred_element_type=jnp.float32
            )
            * scale
        )
        query_grads.append(query_part.reshape(span, head_count * HEAD_DIM))
        key_part = (
            jnp.einsum(
                "kgqs,qkgd->skd",
                grad_scores,
                q_four[offset:finish],
                preferred_element_type=jnp.float32,
            )
            * scale
        )
        grad_keys = grad_keys.at[:finish].add(key_part)
        value_part = jnp.einsum(
            "kgqs,qkgd->skd",
            probs.astype(jnp.bfloat16),
            grad_block,
            preferred_element_type=jnp.float32,
        )
        grad_values = grad_values.at[:finish].add(value_part)
    grad_query_rot = jnp.concatenate(query_grads, axis=0)
    grad_query_lin, grad_query_gain = query_back(grad_query_rot)
    grad_key_lin, grad_key_gain = key_back(grad_keys.reshape(seq_len, kv_count * HEAD_DIM))
    grad_query_b = grad_query_lin.astype(jnp.bfloat16)
    grad_key_b = grad_key_lin.astype(jnp.bfloat16)
    grad_value_b = grad_values.reshape(seq_len, kv_count * HEAD_DIM).astype(jnp.bfloat16)
    grad_w_query = matmul_at(normed_b, grad_query_b)
    grad_w_key = matmul_at(normed_b, grad_key_b)
    grad_w_value = matmul_at(normed_b, grad_value_b)
    grad_normed = lax.psum(
        matmul_bt(grad_query_b, w_query)
        + matmul_bt(grad_key_b, w_key)
        + matmul_bt(grad_value_b, w_value),
        "tensor",
    )
    grad_from_one, grad_attn_gain = norm_back(grad_normed)
    grad_inputs = (grad_middle + grad_from_one).astype(jnp.bfloat16)
    gain_totals = lax.psum((grad_query_gain, grad_key_gain), ("dp", "tensor"))
    summed = (
        lax.psum_scatter(grad_w_query, "dp", scatter_dimension=0, tiled=True),
        lax.psum_scatter(grad_w_key, "dp", scatter_dimension=0, tiled=True),
        lax.psum_scatter(grad_w_value, "dp", scatter_dimension=0, tiled=True),
        lax.psum_scatter(grad_w_output, "dp", scatter_dimension=0, tiled=True),
        lax.psum_scatter(grad_attn_gain, "dp", scatter_dimension=0, tiled=True),
        lax.psum_scatter(grad_w_gate, "dp", scatter_dimension=0, tiled=True),
        lax.psum_scatter(grad_w_up, "dp", scatter_dimension=0, tiled=True),
        lax.psum_scatter(grad_w_down, "dp", scatter_dimension=0, tiled=True),
        lax.psum_scatter(grad_ffn_gain, "dp", scatter_dimension=0, tiled=True),
    )
    (
        sum_query,
        sum_key,
        sum_value,
        sum_output,
        sum_attn_gain,
        sum_gate,
        sum_up,
        sum_down,
        sum_ffn_gain,
    ) = summed
    return (
        block_out,
        grad_inputs,
        sum_attn_gain,
        sum_query,
        sum_key,
        sum_value,
        gain_totals[0],
        gain_totals[1],
        sum_output,
        sum_ffn_gain,
        sum_gate,
        sum_up,
        sum_down,
    )


def solution(mesh):
    placed = (
        P("dp", None),
        P("dp", None),
        P("dp"),
        P(),
        P(None, "tensor"),
        P(None, "tensor"),
        P(None, "tensor"),
        P(),
        P(),
        P(None, "tensor"),
        P(),
        P(None, "tensor"),
        P(None, "tensor"),
        P(None, "tensor"),
    )
    return jax.shard_map(
        per_device,
        mesh=mesh,
        in_specs=placed,
        out_specs=(
            P("dp", None),
            P("dp", None),
            P("dp"),
            P("dp", "tensor"),
            P("dp", "tensor"),
            P("dp", "tensor"),
            P(),
            P(),
            P("dp", "tensor"),
            P("dp"),
            P("dp", "tensor"),
            P("dp", "tensor"),
            P("dp", "tensor"),
        ),
        check_vma=False,
    )
```

profile of v0, /device:TPU:0, one launch (start us, length us, event | category | flops | bytes accessed | tf_op | source)
XLA Modules:
  0.0 1132.0 jit_solution(1060964005794330578)
XLA Ops:
  9.4 2.1 fusion.27
  13.8 2.6 convolution_convert_fusion.1
  24.4 2.1 copy-done.1
  26.5 1.6 fusion.45
  28.1 7.6 fusion.82
  35.7 8.0 fusion.3
  43.7 7.5 fusion.46
  52.0 3.3 fusion.58
  55.4 31.2 %all-reduce.15.cloned.1.call-done = f32[1024,1024]{1,0:T(8,128)} async-done(((f32[1024,1024]{1,0:T(8,128)}), f32[1024,1024]{1,0:T(8,128)}) %all-reduce.15.cloned.1.call-update) | async-done | bytes 4194320 | tf_op jit(solution)/shard_map/psum | solution.py:140
  86.6 2.8 multiply_reduce_fusion.2
  89.9 12.5 %fusion.85 = f32[1024,2304]{1,0:T(8,128)} fusion(bf16[1024,1024]{1,0:T(8,128)(2,1)S(1)} %multiply_convert_fusion.2, bf16[1024,2304]{1,0:T(8,128)(2,1)} %param.38), kind=kOutput, calls=%fused_computation.155 | convolution fusion | flops 4831838208 | bytes 16252928 | tf_op jit(solution)/shard_map/dot_general | solution.py:49
  102.5 7.4 fusion.84
  109.9 17.8 %multiply_convert_fusion = (bf16[1024,2304]{1,0:T(8,128)(2,1)}, bf16[1024,2304]{1,0:T(8,128)(2,1)}, bf16[1024,2304]{1,0:T(8,128)(2,1)}) fusion(f32[1024,2304]{1,0:T(8,128)} %fusion.84, f32[1024,2304]{1,0:T(8,128)} %fusion.85, bf16[1024,1024]{1,0:T(8,128)(2,1)S(1)} %copy-done.33, bf16[1024,2304]{1,0:T(8,128)(2,1)} %param.39), kind=kOutput, calls=%fused_computation.15 | convolution fusion | flops 4869586944 | bytes 39845888 | tf_op jit(solution)/shard_map/dot_general | solution.py:49
  127.7 7.1 fusion.87
  134.8 9.1 convolution_add_fusion
  144.0 9.9 fusion.86
  153.9 19.8 %all-reduce.17.cloned.1.call-done = f32[1024,1024]{1,0:T(8,128)} async-done(((f32[1024,1024]{1,0:T(8,128)}), f32[1024,1024]{1,0:T(8,128)}) %all-reduce.17.cloned.1.call-update) | async-done | bytes 4194320 | tf_op jit(solution)/shard_map/psum | solution.py:157
  173.7 4.6 multiply_reduce_fusion
  178.3 3.3 fusion.22
  183.6 2.2 fusion.47
  185.8 5.1 fusion.11
  191.0 4.8 fusion.13
  197.6 1.9 convolution_multiply_fusion.1
  200.1 8.1 fusion
  208.2 4.0 fusion.42
  212.3 4.0 fusion.89
  216.2 8.3 fusion.2
  226.2 2.6 fusion.38
  235.0 3.3 add_add_fusion.2
  239.9 3.0 fusion.69
  243.4 3.0 fusion.71
  246.5 5.9 fusion.54
  252.5 4.3 fusion.73
  256.9 10.3 convolution_bitcast_fusion
  267.1 10.3 copy.70
  277.6 10.1 fusion.91
  287.7 10.2 fusion.90
  299.8 40.9 %all-reduce.8 = (f32[64]{0:T(128)}, f32[64]{0:T(128)}) all-reduce(f32[64]{0:T(128)S(1)} %get-tuple-element.120, f32[64]{0:T(128)S(1)} %get-tuple-element.122), channel_id=1, replica_groups=mesh['dp'=16,'tensor'=2] {'dp','tensor'}, use_global_device_ids=true, to_apply=%region_26.27 | all-reduce | flops 128 | bytes 1024 | tf_op jit(solution)/shard_map/psum | solution.py:221
  340.7 3.6 fusion.21
  344.3 41.4 %all-reduce.9 = (f32[1024]{0:T(1024)S(1)}, f32[1024]{0:T(1024)S(1)}) all-reduce(f32[1024]{0:T(1024)S(1)} %get-tuple-element.118, f32[1024]{0:T(1024)S(1)} %get-tuple-element.116), channel_id=2, replica_groups=mesh['dp'=16,'tensor'=2] {'dp'}, use_global_device_ids=true, to_apply=%region_21.22.clone | all-reduce | flops 2048 | bytes 16384
  386.9 5.7 add_convert_fusion
  393.6 2.3 fusion.24
  395.9 41.5 %reduce-scatter.12.cloned.1.call-done = f32[64,256]{1,0:T(8,128)} async-done(((f32[1024,256]{1,0:T(8,128)}), f32[64,256]{1,0:T(8,128)}) %reduce-scatter.12.cloned.1.call-update) | async-done | bytes 65552 | tf_op jit(solution)/shard_map/reduce_scatter | solution.py:224
  437.4 79.6 %reduce-scatter.16.cloned.1.call-done = f32[64,512]{1,0:T(8,128)} async-done(((f32[1024,512]{1,0:T(8,128)}), f32[64,512]{1,0:T(8,128)}) %reduce-scatter.16.cloned.1.call-update) | async-done | bytes 131088 | tf_op jit(solution)/shard_map/reduce_scatter | solution.py:226
  517.0 80.6 %reduce-scatter.10.cloned.1.call-done = f32[64,512]{1,0:T(8,128)} async-done(((f32[1024,512]{1,0:T(8,128)}), f32[64,512]{1,0:T(8,128)}) %reduce-scatter.10.cloned.1.call-update) | async-done | bytes 131088 | tf_op jit(solution)/shard_map/reduce_scatter | solution.py:223
  597.6 174.4 %reduce-scatter.22.cloned.1.call-done = f32[64,2304]{1,0:T(8,128)} async-done(((f32[1024,2304]{1,0:T(8,128)}), f32[64,2304]{1,0:T(8,128)}) %reduce-scatter.22.cloned.1.call-update) | async-done | bytes 589840
  771.9 177.1 %reduce-scatter.20.cloned.1.call-done = f32[64,2304]{1,0:T(8,128)} async-done(((f32[1024,2304]{1,0:T(8,128)}), f32[64,2304]{1,0:T(8,128)}) %reduce-scatter.20.cloned.1.call-update) | async-done | bytes 589840 | tf_op jit(solution)/shard_map/reduce_scatter | solution.py:229
  949.0 176.1 %reduce-scatter.18.cloned.1.call-done = f32[64,2304]{1,0:T(8,128)} async-done(((f32[1024,2304]{1,0:T(8,128)}), f32[64,2304]{1,0:T(8,128)}) %reduce-scatter.18.cloned.1.call-update) | async-done | bytes 589840 | tf_op jit(solution)/shard_map/reduce_scatter | solution.py:228
  (218 shorter events, 30.7 us)
Async XLA Ops:
  7.2 10.3 copy-start
  7.2 9.3 copy-start.6
  7.2 9.2 copy-start.55
  7.2 79.4 %all-reduce.15.cloned.1.call-start = ((), (), s32[]{:S(2)}) async-start(), calls=%async_computation.7 | async-start | bytes 8388608 | tf_op jit(solution)/shard_map/psum | solution.py:140
  11.5 6.0 copy-start.50
  13.4 3.1 copy-start.38
  16.4 27.3 %copy-start.34 = (bf16[1024,256]{0,1:T(8,128)(2,1)}, bf16[1024,256]{0,1:T(8,128)(2,1)S(1)}, u32[]{:S(2)}) copy-start(bf16[1024,256]{0,1:T(8,128)(2,1)S(1)} %convolution_convert_fusion.1) | copy-start | bytes 1572868
  20.0 8.0 copy-start.25
  20.0 8.0 copy-start.27
  21.6 6.5 copy-start.30
  23.2 3.3 copy-start.1
  28.1 23.1 %copy-start.40 = (bf16[4,64,2,512]{3,1,2,0:T(8,128)(2,1)}, bf16[4,64,2,512]{3,1,2,0:T(8,128)(2,1)S(1)}, u32[]{:S(2)}) copy-start(bf16[4,64,2,512]{3,1,2,0:T(8,128)(2,1)S(1)} %fusion.45) | copy-start | bytes 1572868
  43.7 8.3 copy-start.61
  55.4 34.1 %copy-start.54 = (f32[1024]{0:T(1024)S(1)}, f32[1024]{0:T(1024)}, u32[]{:S(2)}) copy-start(f32[1024]{0:T(1024)} %param.36) | copy-start | bytes 12292
  55.4 118.3 %all-reduce.17.cloned.1.call-start = ((), (), s32[]{:S(2)}) async-start(), calls=%async_computation.8 | async-start | bytes 8388608 | tf_op jit(solution)/shard_map/psum | solution.py:157
  89.4 13.0 %copy-start.2 = (f32[1024,1024]{1,0:T(8,128)}, f32[1024,1024]{1,0:T(8,128)S(1)}, u32[]{:S(2)}) copy-start(f32[1024,1024]{1,0:T(8,128)S(1)} %get-tuple-element.131) | copy-start | bytes 12582916
  89.5 13.0 %slice-start.6 = ((s8[4718592]{0:T(1024)(128)(4,1)}), s8[4194304]{0:T(1024)(128)(4,1)S(1)}, s32[]{:S(2)}) async-start(s8[4718592]{0:T(1024)(128)(4,1)} %bitcast.220), calls=%async_computation.23 | async-start | bytes 8388608
  89.9 12.5 %copy-start.29 = (bf16[1024,1024]{1,0:T(8,128)(2,1)}, bf16[1024,1024]{1,0:T(8,128)(2,1)S(1)}, u32[]{:S(2)}) copy-start(bf16[1024,1024]{1,0:T(8,128)(2,1)S(1)} %multiply_convert_fusion.2) | copy-start | bytes 6291460
  89.9 12.5 %slice-start.7 = ((s8[4718592]{0:T(1024)(128)(4,1)}), s8[524288]{0:T(1024)(128)(4,1)S(1)}, s32[]{:S(2)}) async-start(s8[4718592]{0:T(1024)(128)(4,1)} %bitcast.220), calls=%async_computation.24 | async-start | bytes 1048576
  102.5 7.5 copy-start.33
  127.7 7.1 copy-start.64
  143.9 196.8 %all-reduce.19.cloned.1.call-start = ((), (), s32[]{:S(2)}) async-start(), calls=%async_computation.16 | async-start | bytes 16777216 | tf_op jit(solution)/shard_map/psum | solution.py:148
  173.7 4.6 copy-start.3
  173.7 9.9 slice-start.4
  178.3 3.3 copy-start.62
  178.3 5.3 slice-start.5
  190.9 4.9 copy-start.15
  190.9 8.6 slice-start
  190.9 8.6 slice-start.1
  191.0 8.6 slice-start.2
  195.8 4.1 slice-start.3
  212.3 12.3 %copy-start.18 = (bf16[1024,4,64]{0,2,1:T(8,128)(2,1)}, bf16[1024,4,64]{0,2,1:T(8,128)(2,1)S(1)}, u32[]{:S(2)}) copy-start(bf16[1024,4,64]{0,2,1:T(8,128)(2,1)S(1)} %fusion.42) | copy-start | bytes 1572868
  212.3 4.0 copy-start.46
  216.2 8.3 copy-start.26
  216.2 8.3 copy-start.28
  226.2 2.9 copy-start.13
  226.2 2.9 copy-start.43
  229.9 3.0 copy-start.32
  238.4 157.6 %reduce-scatter.14.cloned.1.call-start = ((), (), s32[]{:S(2)}) async-start(), calls=%async_computation.11 | async-start | bytes 1114112 | tf_op jit(solution)/shard_map/reduce_scatter | solution.py:225
  243.0 194.4 %reduce-scatter.12.cloned.1.call-start = ((), (), s32[]{:S(2)}) async-start(), calls=%async_computation.10 | async-start | bytes 1114112 | tf_op jit(solution)/shard_map/reduce_scatter | solution.py:224
  246.5 270.5 %reduce-scatter.16.cloned.1.call-start = ((), (), s32[]{:S(2)}) async-start(), calls=%async_computation.12 | async-start | bytes 2228224 | tf_op jit(solution)/shard_map/reduce_scatter | solution.py:226
  252.5 345.1 %reduce-scatter.10.cloned.1.call-start = ((), (), s32[]{:S(2)}) async-start(), calls=%async_computation.9 | async-start | bytes 2228224 | tf_op jit(solution)/shard_map/reduce_scatter | solution.py:223
  256.8 515.1 %reduce-scatter.22.cloned.1.call-start = ((), (), s32[]{:S(2)}) async-start(), calls=%async_computation.15 | async-start | bytes 10027008
  277.5 671.5 %reduce-scatter.20.cloned.1.call-start = ((), (), s32[]{:S(2)}) async-start(), calls=%async_computation.14 | async-start | bytes 10027008 | tf_op jit(solution)/shard_map/reduce_scatter | solution.py:229
  287.7 837.3 %reduce-scatter.18.cloned.1.call-start = ((), (), s32[]{:S(2)}) async-start(), calls=%async_computation.13 | async-start | bytes 10027008 | tf_op jit(solution)/shard_map/reduce_scatter | solution.py:228
  297.9 89.0 %copy-start.53 = (f32[1024]{0:T(1024)S(1)}, f32[1024]{0:T(1024)}, u32[]{:S(2)}) copy-start(f32[1024]{0:T(1024)} %copy-done.52) | copy-start | bytes 12292
  386.9 5.7 copy-start.5
  386.9 6.7 copy-start.11
  (35 other events, 62.5 us)
Sparse Core Ops, SparseCore 0:
  55.5 31.1 all-reduce.14
  144.0 29.5 all-reduce.16
  238.5 40.0 all-reduce.18
  281.3 78.9 reduce-scatter.13
  363.1 74.2 reduce-scatter.11
  440.1 76.8 reduce-scatter.15
  519.8 77.6 reduce-scatter.9
  603.8 168.0 reduce-scatter.21
  779.1 169.7 reduce-scatter.19
  955.1 169.9 reduce-scatter.17
where the time goes:
time: 1140 us; the launch traced here: 1130 us
  waiting for transfers between devices  780 us (68%)
  matrix products  173 us (15%)
  blocking collectives  82.3 us (7%)
  other arithmetic  54.3 us (5%)
  local copies, waits for them, and re-layouts  24.3 us (2%)
  between operations  16.8 us (1%)
    reduce_scatter x1, waiting for transfers between devices, per_device(): lax.psum_scatter(grad_w_up, 'dp', scatter_dimension=0, tiled=True)  177 us
    reduce_scatter x1, waiting for transfers between devices, per_device(): lax.psum_scatter(grad_w_gate, 'dp', scatter_dimension=0, tiled=True)  176 us
    unnamed x11, waiting for transfers between devices  175 us
    reduce_scatter x1, waiting for transfers between devices, per_device(): lax.psum_scatter(grad_w_query, 'dp', scatter_dimension=0, tiled=True)  80.6 us
    reduce_scatter x1, waiting for transfers between devices, per_device(): lax.psum_scatter(grad_w_output, 'dp', scatter_dimension=0, tiled=True)  79.6 us
    dot_general x7, matrix products, matmul_at(): lax.dot_general(left, right, (((0,), (0,)), ((), ())), preferred_element_...  46.8 us
    dot_general x7, matrix products, matmul(): return jnp.dot(left, right, preferred_element_type=jnp.float32)  44 us
    reduce_scatter x1, waiting for transfers between devices, per_device(): lax.psum_scatter(grad_w_key, 'dp', scatter_dimension=0, tiled=True)  41.5 us
  transfers between devices with their start and end apart: 10, of which 8 were waited for; matrix products, arithmetic and copies ran while one was open for 7% of the time, Pallas kernels for 0%

commit v1 on v0

--- a/solution.py
+++ b/solution.py
@@ -59,6 +59,59 @@
     return lax.dot_general(
         left, right, (((0,), (0,)), ((), ())), preferred_element_type=jnp.float32
     )
+
+
+def swap_add(values):
+    pairs = [(0, 1), (1, 0)]
+    return values + lax.ppermute(values, "tensor", pairs)
+
+
+def bit_orders(bits):
+    if bits == 4:
+        return ((0, 1, 2, 3), (1, 2, 0, 3), (2, 0, 1, 3))
+    names = tuple(range(bits))
+    return tuple(names[turn % bits :] + names[: turn % bits] for turn in range(3))
+
+
+def halving_scatter(values, order):
+    devices = lax.axis_size("dp")
+    me = lax.axis_index("dp")
+    rows, columns = values.shape
+    bits = len(order)
+    addends = [values.reshape((2,) * bits + (rows // devices, columns))]
+    left = list(range(bits - 1, -1, -1))
+    for bit in order:
+        axis = left.index(bit)
+        mine = (me >> bit) & 1
+
+        def take(array, which):
+            return lax.dynamic_index_in_dim(array, which, axis, keepdims=False)
+
+        send = sum(take(item, 1 - mine) for item in addends[1:]) + take(addends[0], 1 - mine)
+        pairs = [(i, i ^ (1 << bit)) for i in range(devices)]
+        received = lax.ppermute(send, "dp", pairs)
+        addends = [take(item, mine) for item in addends] + [received]
+        left.remove(bit)
+    return sum(addends[1:]) + addends[0]
+
+
+def cut_points(columns):
+    tiles = columns // 128
+    if tiles < 3:
+        return [0, columns]
+    one = -(-tiles // 3)
+    return [0, one * 128, min(2 * one, tiles) * 128, columns] if 2 * one < tiles else [0, one * 128, columns]
+
+
+def scatter_weight(values):
+    devices = lax.axis_size("dp")
+    orders = bit_orders(devices.bit_length() - 1)
+    cuts = cut_points(values.shape[1])
+    parts = [
+        halving_scatter(values[:, low:high], orders[turn % 3])
+        for turn, (low, high) in enumerate(zip(cuts[:-1], cuts[1:]))
+    ]
+    return jnp.concatenate(parts, axis=1)
 
 
 def per_device(
@@ -137,7 +190,7 @@
         )
         pieces.append(mixed_part.reshape(span, head_count * HEAD_DIM))
     mixed_b = jnp.concatenate(pieces, axis=0).astype(jnp.bfloat16)
-    attn_out = lax.psum(matmul_bt(mixed_b, w_output), "tensor")
+    attn_out = swap_add(matmul_bt(mixed_b, w_output))
     middle = input_full + attn_out
     normed_two, norm_two_back = jax.vjp(rms_scale, middle, ffn_gain)
     normed_two_b = normed_two.astype(jnp.bfloat16)
@@ -145,7 +198,7 @@
     upper = matmul(normed_two_b, w_up)
     hidden, swish_back = jax.vjp(lambda left, right: jax.nn.silu(left) * right, gate, upper)
     hidden_b = hidden.astype(jnp.bfloat16)
-    ffn_out = lax.psum(matmul_bt(hidden_b, w_down), "tensor")
+    ffn_out = swap_add(matmul_bt(hidden_b, w_down))
     block_out = (middle + ffn_out).astype(jnp.bfloat16)
     grad_w_down = matmul_at(cotangent, hidden_b)
     grad_hidden = matmul(cotangent, w_down)
@@ -154,8 +207,8 @@
     grad_upper_b = grad_upper.astype(jnp.bfloat16)
     grad_w_gate = matmul_at(normed_two_b, grad_gate_b)
     grad_w_up = matmul_at(normed_two_b, grad_upper_b)
-    grad_normed_two = lax.psum(
-        matmul_bt(grad_gate_b, w_gate) + matmul_bt(grad_upper_b, w_up), "tensor"
+    grad_normed_two = swap_add(
+        matmul_bt(grad_gate_b, w_gate) + matmul_bt(grad_upper_b, w_up)
     )
     grad_from_two, grad_ffn_gain = norm_two_back(grad_normed_two)
     grad_middle = cotangent.astype(jnp.float32) + grad_from_two
@@ -210,37 +263,26 @@
     grad_w_query = matmul_at(normed_b, grad_query_b)
     grad_w_key = matmul_at(normed_b, grad_key_b)
     grad_w_value = matmul_at(normed_b, grad_value_b)
-    grad_normed = lax.psum(
+    grad_normed = swap_add(
         matmul_bt(grad_query_b, w_query)
         + matmul_bt(grad_key_b, w_key)
-        + matmul_bt(grad_value_b, w_value),
-        "tensor",
+        + matmul_bt(grad_value_b, w_value)
     )
     grad_from_one, grad_attn_gain = norm_back(grad_normed)
     grad_inputs = (grad_middle + grad_from_one).astype(jnp.bfloat16)
     gain_totals = lax.psum((grad_query_gain, grad_key_gain), ("dp", "tensor"))
-    summed = (
-        lax.psum_scatter(grad_w_query, "dp", scatter_dimension=0, tiled=True),
-        lax.psum_scatter(grad_w_key, "dp", scatter_dimension=0, tiled=True),
-        lax.psum_scatter(grad_w_value, "dp", scatter_dimension=0, tiled=True),
-        lax.psum_scatter(grad_w_output, "dp", scatter_dimension=0, tiled=True),
-        lax.psum_scatter(grad_attn_gain, "dp", scatter_dimension=0, tiled=True),
-        lax.psum_scatter(grad_w_gate, "dp", scatter_dimension=0, tiled=True),
-        lax.psum_scatter(grad_w_up, "dp", scatter_dimension=0, tiled=True),
-        lax.psum_scatter(grad_w_down, "dp", scatter_dimension=0, tiled=True),
-        lax.psum_scatter(grad_ffn_gain, "dp", scatter_dimension=0, tiled=True),
-    )
-    (
-        sum_query,
-        sum_key,
-        sum_value,
-        sum_output,
-        sum_attn_gain,
-        sum_gate,
-        sum_up,
-        sum_down,
-        sum_ffn_gain,
-    ) = summed
+    grad_three = jnp.concatenate([grad_w_query, grad_w_key, grad_w_value], axis=1)
+    sum_down = scatter_weight(grad_w_down)
+    sum_gate = scatter_weight(grad_w_gate)
+    sum_up = scatter_weight(grad_w_up)
+    sum_output = scatter_weight(grad_w_output)
+    sum_three = scatter_weight(grad_three)
+    q_width, k_width = w_query.shape[1], w_key.shape[1]
+    sum_query = sum_three[:, :q_width]
+    sum_key = sum_three[:, q_width : q_width + k_width]
+    sum_value = sum_three[:, q_width + k_width :]
+    sum_attn_gain = lax.psum_scatter(grad_attn_gain, "dp", scatter_dimension=0, tiled=True)
+    sum_ffn_gain = lax.psum_scatter(grad_ffn_gain, "dp", scatter_dimension=0, tiled=True)
     return (
         block_out,
         grad_inputs,

time: 1140 us -> 652 us (0.57)
  waiting for transfers between devices: 780 us -> 155 us
  starting transfers between devices: 0.82 us -> 67 us
  other arithmetic: 54.3 us -> 116 us
  local copies, waits for them, and re-layouts: 24.3 us -> 57.5 us
  between operations: 16.8 us -> 3.78 us
  matrix products: 173 us -> 161 us
    reduce_scatter x6 -> x0, waiting for transfers between devices: 555 us -> none  [the longest x1 177 us: per_device(): lax.psum_scatter(grad_w_up, 'dp', scatter_dimension=0, tiled=True)]
    unnamed x11 -> x0, waiting for transfers between devices: 175 us -> none
    ppermute x0 -> x60, waiting for transfers between devices: none -> 155 us  [the longest x56 155 us: halving_scatter(): received = lax.ppermute(send, 'dp', pairs)]
    ppermute x0 -> x60, starting transfers between devices: none -> 67 us  [the longest x56 66.4 us: halving_scatter(): received = lax.ppermute(send, 'dp', pairs)]
    add x0 -> x56, other arithmetic: none -> 53.7 us  [the longest x42 39.8 us: halving_scatter(): sum((take(item, 1 - mine) for item in addends[1:]))]
    psum x3 -> x0, waiting for transfers between devices: 51 us -> none  [the longest x1 31.2 us: per_device(): attn_out = lax.psum(matmul_bt(mixed_b, w_output), 'tensor')]
    squeeze x0 -> x14, local copies, waits for them, and re-layouts: none -> 16.4 us  [take(): return lax.dynamic_index_in_dim(array, which, axis, keepdims=False)]
    slice x0 -> x5, local copies, waits for them, and re-layouts: none -> 13.9 us  [the longest x4 13.3 us: scatter_weight(): values[:, low:high]]
  transfers between devices with their start and end apart: 10 -> 60, of which waited for: 8 -> 26; matrix products, arithmetic and copies ran while one was open for 7% -> 25% of each run, Pallas kernels for 0% -> 0%
where the time goes in v1:
time: 652 us; the launch traced here: 642 us
  matrix products  161 us (25%)
  waiting for transfers between devices  155 us (24%)
  other arithmetic  116 us (18%)
  blocking collectives  82.5 us (13%)
  starting transfers between devices  67 us (10%)
  local copies, waits for them, and re-layouts  57.5 us (9%)
    ppermute x56, waiting for transfers between devices, halving_scatter(): received = lax.ppermute(send, 'dp', pairs)  155 us
    ppermute x56, starting transfers between devices, halving_scatter(): received = lax.ppermute(send, 'dp', pairs)  66.4 us
    dot_general x7, matrix products, matmul(): return jnp.dot(left, right, preferred_element_type=jnp.float32)  44.9 us
    psum x1, blocking collectives, per_device(): gain_totals = lax.psum((grad_query_gain, grad_key_gain), ('dp', 'tensor'))  43.9 us
    add x42, other arithmetic, halving_scatter(): sum((take(item, 1 - mine) for item in addends[1:]))  39.8 us
    unnamed x1, blocking collectives  38.6 us
    dot_general x7, matrix products, matmul_bt(): lax.dot_general(left, right, (((1,), (1,)), ((), ())), preferred_element_...  37.9 us
    dot_general x7, matrix products, matmul_at(): lax.dot_general(left, right, (((0,), (0,)), ((), ())), preferred_element_...  33.8 us
  transfers between devices with their start and end apart: 60, of which 26 were waited for; matrix products, arithmetic and copies ran while one was open for 25% of the time, Pallas kernels for 0%

profile of v1, /device:TPU:0, one launch (start us, length us, event | category | flops | bytes accessed | tf_op | source)
XLA Modules:
  0.0 642.3 jit_solution(16958741868771908722)
XLA Ops:
  25.4 7.5 %fusion.90 = (f32[4,2,512]{2,1,0:T(2,128)S(1)}, f32[4,2,512,1024]{2,3,1,0:T(8,128)}) fusion(bf16[512,4,2,64]{0,3,2,1:T(8,128)(2,1)S(1)} %bitcast.846, pred[512,1024]{0,1:T(8,128)(4,1)S(1)} %fusion.32, bf16[1024,4,32]{0,2,1:T(8,128)(2,1)S(1)} %get-tuple-element.155, bf16[1024,4,32]{0,2,1:T(8,128)(2,1)S(1)} %get-tuple-element.154), kind=kOutput, calls=%fused_computation.312 | convolution fusion | flops 550498304 | bytes 18366464 | tf_op jit(solution)/shard_map/qkgd,skd->kgqs/dot_general | solution.py:159
  33.0 8.0 %fusion.3 = f32[4,2,512]{2,1,0:T(2,128)S(1)} fusion(f32[4,2,512,1024]{2,3,1,0:T(8,128)} %get-tuple-element.169, f32[4,2,512]{2,1,0:T(2,128)S(1)} %get-tuple-element.168), kind=kLoop, calls=%fused_computation.9 | loop fusion | flops 8384512 | bytes 16809984 | tf_op jit(solution)/shard_map/reduce_sum | solution.py:182
  41.0 7.5 %fusion.46 = bf16[4,64,2,512]{3,1,2,0:T(8,128)(2,1)S(1)} fusion(bf16[1024,4,64,1]{0,2,3,1:T(8,128)(2,1)S(1)} %bitcast.852, f32[4,2,512,1024]{2,3,1,0:T(8,128)} %get-tuple-element.169, f32[4,2,512]{2,1,0:T(2,128)S(1)} %fusion.3, f32[4,2,512]{2,1,0:T(2,128)S(1)} %get-tuple-element.168), kind=kOutput, calls=%fused_computation.94 | convolution fusion | flops 549715968 | bytes 17858560 | tf_op jit(solution)/shard_map/kgqs,skd->qkgd/dot_general | solution.py:185
  48.5 3.3 fusion.58
  52.3 3.9 copy.74
  58.6 10.1 %fusion.94 = f32[1024,2304]{1,0:T(8,128)} fusion(bf16[1024,1024]{1,0:T(8,128)(2,1)} %param.27, bf16[1024,2304]{1,0:T(8,128)(2,1)} %param.39), kind=kOutput, calls=%fused_computation.316 | convolution fusion | flops 4831838208 | bytes 16252928 | tf_op jit(solution)/shard_map/dot_general | solution.py:49
  68.8 4.7 multiply_reduce_fusion.2
  73.9 10.3 %fusion.92 = f32[1024,2304]{1,0:T(8,128)} fusion(bf16[1024,1024]{0,1:T(8,128)(2,1)S(1)} %multiply_convert_fusion.2, bf16[1024,2304]{1,0:T(8,128)(2,1)} %param.38), kind=kOutput, calls=%fused_computation.314 | convolution fusion | flops 4831838208 | bytes 16252928 | tf_op jit(solution)/shard_map/dot_general | solution.py:49
  84.3 17.6 %multiply_convert_fusion = (bf16[1024,2304]{1,0:T(8,128)(2,1)}, bf16[1024,2304]{1,0:T(8,128)(2,1)}, bf16[1024,2304]{1,0:T(8,128)(2,1)}) fusion(f32[1024,2304]{1,0:T(8,128)} %fusion.94, f32[1024,2304]{1,0:T(8,128)} %fusion.92, bf16[1024,1024]{0,1:T(8,128)(2,1)S(1)} %multiply_convert_fusion.2, bf16[1024,2304]{1,0:T(8,128)(2,1)} %param.37), kind=kOutput, calls=%fused_computation.15 | convolution fusion | flops 4869586944 | bytes 39845888 | tf_op jit(solution)/shard_map/dot_general | solution.py:49
  101.9 10.0 %convolution_bitcast_fusion = f32[1024,2304]{1,0:T(8,128)} fusion(bf16[1024,2304]{1,0:T(8,128)(2,1)} %get-tuple-element.132, bf16[1024,1024]{1,0:T(8,128)(2,1)S(1)} %copy-done.44), kind=kOutput, calls=%fused_computation.37 | convolution fusion | flops 4831838208 | bytes 16252928 | tf_op jit(solution)/shard_map/dot_general | solution.py:59
  111.9 4.4 fusion.83
  125.9 7.6 %fusion.100 = f32[1024,2304]{1,0:T(8,128)} fusion(bf16[1024,1024]{0,1:T(8,128)(2,1)S(1)} %multiply_convert_fusion.2, bf16[1024,2304]{1,0:T(8,128)(2,1)S(1)} %copy-done.93), kind=kOutput, calls=%fused_computation.322 | convolution fusion | flops 4831838208 | bytes 16252928 | tf_op jit(solution)/shard_map/dot_general | solution.py:59
  133.5 4.4 fusion.84
  144.6 9.8 %fusion.99 = f32[1024,2304]{1,0:T(8,128)} fusion(bf16[1024,1024]{0,1:T(8,128)(2,1)S(1)} %multiply_convert_fusion.2, bf16[1024,2304]{1,0:T(8,128)(2,1)} %get-tuple-element.131), kind=kOutput, calls=%fused_computation.321 | convolution fusion | flops 4831838208 | bytes 16252928 | tf_op jit(solution)/shard_map/dot_general | solution.py:59
  154.5 4.4 fusion.85
  162.9 9.7 %fusion.95 = f32[1024,1024]{0,1:T(8,128)} fusion(bf16[1024,2304]{1,0:T(8,128)(2,1)} %get-tuple-element.131, bf16[1024,2304]{1,0:T(8,128)(2,1)} %param.37), kind=kOutput, calls=%fused_computation.317 | convolution fusion | flops 4831838208 | bytes 13631488 | tf_op jit(solution)/shard_map/dot_general | solution.py:53
  173.9 15.5 %collective-permute-done.36 = f32[2,2,2,64,768]{4,3,2,1,0:T(8,128)} collective-permute-done((f32[2,2,2,64,768]{4,3,2,1,0:T(8,128)}, f32[2,2,2,64,768]{4,3,2,1,0:T(8,128)}, u32[]{:S(2)}, u32[]{:S(2)}) %collective-permute-start.36) | collective-permute-done | bytes 1572896 | tf_op jit(solution)/shard_map/ppermute | solution.py:92
  191.4 8.3 %convolution_add_fusion = f32[1024,1024]{0,1:T(8,128)S(1)} fusion(f32[1024,1024]{0,1:T(8,128)} %fusion.95, bf16[1024,2304]{1,0:T(8,128)(2,1)} %get-tuple-element.130, bf16[1024,2304]{1,0:T(8,128)(2,1)S(1)} %bitcast.870), kind=kOutput, calls=%fused_computation.70 | convolution fusion | flops 4832886784 | bytes 17825792 | tf_op jit(solution)/shard_map/dot_general | solution.py:53
  210.9 11.9 %collective-permute-done.24 = f32[2,2,2,64,768]{4,3,2,1,0:T(8,128)S(1)} collective-permute-done((f32[2,2,2,64,768]{4,3,2,1,0:T(8,128)}, f32[2,2,2,64,768]{4,3,2,1,0:T(8,128)S(1)}, u32[]{:S(2)}, u32[]{:S(2)}) %collective-permute-start.24) | collective-permute-done | bytes 1572896 | tf_op jit(solution)/shard_map/ppermute | solution.py:92
  228.9 9.8 %fusion.93 = f32[1024,1024]{0,1:T(8,128)} fusion(bf16[1024,2304]{1,0:T(8,128)(2,1)} %get-tuple-element.132, bf16[1024,2304]{1,0:T(8,128)(2,1)} %param.39), kind=kOutput, calls=%fused_computation.315 | convolution fusion | flops 4831838208 | bytes 13631488 | tf_op jit(solution)/shard_map/dot_general | solution.py:53
  239.0 5.2 collective-permute-done.32
  247.7 13.5 %collective-permute-done.53 = f32[2,2,64,768]{3,2,1,0:T(8,128)} collective-permute-done((f32[2,2,64,768]{3,2,1,0:T(8,128)}, f32[2,2,64,768]{3,2,1,0:T(8,128)}, u32[]{:S(2)}, u32[]{:S(2)}) %collective-permute-start.53) | collective-permute-done | bytes 786464 | tf_op jit(solution)/shard_map/ppermute | solution.py:92
  271.0 6.9 %collective-permute-done.41 = f32[2,2,64,768]{3,2,1,0:T(8,128)S(1)} collective-permute-done((f32[2,2,64,768]{3,2,1,0:T(8,128)S(1)}, f32[2,2,64,768]{3,2,1,0:T(8,128)S(1)}, u32[]{:S(2)}, u32[]{:S(2)}) %collective-permute-start.41) | collective-permute-done | bytes 786464 | tf_op jit(solution)/shard_map/ppermute | solution.py:92
  282.4 12.3 %collective-permute-done.29 = f32[2,2,64,768]{3,2,1,0:T(8,128)S(1)} collective-permute-done((f32[2,2,64,768]{3,2,1,0:T(8,128)S(1)}, f32[2,2,64,768]{3,2,1,0:T(8,128)S(1)}, u32[]{:S(2)}, u32[]{:S(2)}) %collective-permute-start.29) | collective-permute-done | bytes 786464 | tf_op jit(solution)/shard_map/ppermute | solution.py:92
  298.1 5.1 collective-permute-done.50
  314.9 3.8 collective-permute-done.26
  329.3 8.6 %collective-permute-done.51 = f32[64,768]{1,0:T(8,128)S(1)} collective-permute-done((f32[64,768]{1,0:T(8,128)S(1)}, f32[64,768]{1,0:T(8,128)S(1)}, u32[]{:S(2)}, u32[]{:S(2)}) %collective-permute-start.51) | collective-permute-done | bytes 196640 | tf_op jit(solution)/shard_map/ppermute | solution.py:92
  339.0 7.3 %collective-permute-done.55 = f32[64,768]{1,0:T(8,128)S(1)} collective-permute-done((f32[64,768]{1,0:T(8,128)S(1)}, f32[64,768]{1,0:T(8,128)S(1)}, u32[]{:S(2)}, u32[]{:S(2)}) %collective-permute-start.55) | collective-permute-done | bytes 196640 | tf_op jit(solution)/shard_map/ppermute | solution.py:92
  347.4 7.3 %collective-permute-done.59 = f32[64,768]{1,0:T(8,128)S(1)} collective-permute-done((f32[64,768]{1,0:T(8,128)S(1)}, f32[64,768]{1,0:T(8,128)S(1)}, u32[]{:S(2)}, u32[]{:S(2)}) %collective-permute-start.59) | collective-permute-done | bytes 196640 | tf_op jit(solution)/shard_map/ppermute | solution.py:92
  355.8 7.3 %collective-permute-done.39 = f32[64,768]{1,0:T(8,128)S(1)} collective-permute-done((f32[64,768]{1,0:T(8,128)S(1)}, f32[64,768]{1,0:T(8,128)S(1)}, u32[]{:S(2)}, u32[]{:S(2)}) %collective-permute-start.39) | collective-permute-done | bytes 196640 | tf_op jit(solution)/shard_map/ppermute | solution.py:92
  364.1 7.4 %collective-permute-done.43 = f32[64,768]{1,0:T(8,128)S(1)} collective-permute-done((f32[64,768]{1,0:T(8,128)S(1)}, f32[64,768]{1,0:T(8,128)S(1)}, u32[]{:S(2)}, u32[]{:S(2)}) %collective-permute-start.43) | collective-permute-done | bytes 196640 | tf_op jit(solution)/shard_map/ppermute | solution.py:92
  371.6 8.4 %collective-permute-done.47 = f32[64,768]{1,0:T(8,128)S(1)} collective-permute-done((f32[64,768]{1,0:T(8,128)S(1)}, f32[64,768]{1,0:T(8,128)S(1)}, u32[]{:S(2)}, u32[]{:S(2)}) %collective-permute-start.47) | collective-permute-done | bytes 196640 | tf_op jit(solution)/shard_map/ppermute | solution.py:92
  380.0 8.4 %collective-permute-done.27 = f32[64,768]{1,0:T(8,128)S(1)} collective-permute-done((f32[64,768]{1,0:T(8,128)S(1)}, f32[64,768]{1,0:T(8,128)S(1)}, u32[]{:S(2)}, u32[]{:S(2)}) %collective-permute-start.27) | collective-permute-done | bytes 196640 | tf_op jit(solution)/shard_map/ppermute | solution.py:92
  393.4 3.2 collective-permute-done.35
  401.5 6.7 %fusion.22 = (f32[1024,1024]{0,1:T(8,128)S(1)}, bf16[1024,1024]{0,1:T(8,128)(2,1)}) fusion(f32[1024,1024]{0,1:T(8,128)S(1)} %get-tuple-element.129, bf16[1024,1024]{0,1:T(8,128)(2,1)S(1)} %copy-done.21, f32[1024]{0:T(1024)S(1)} %multiply_multiply_fusion.5, f32[1024]{0:T(1024)S(1)} %copy-done.85, f32[1024]{0:T(1024)S(1)} %fusion.80, ...), kind=kLoop, calls=%fused_computation.45 | loop fusion | flops 11534336 | bytes 29372416 | tf_op jit(solution)/shard_map/add | solution.py:214
  425.5 7.6 %fusion = (f32[4,2,512]{2,1,0:T(2,128)S(1)}, f32[4,1024,512,2]{2,1,3,0:T(8,128)}) fusion(f32[4,2,512,1024]{2,3,1,0:T(8,128)S(1)} %bitcast.763, f32[4,2,512]{2,1,0:T(2,128)S(1)} %bitcast.858, bf16[1024,4,64,1]{0,2,3,1:T(8,128)(2,1)S(1)} %bitcast.853, bf16[512,4,2,64]{0,3,2,1:T(8,128)(2,1)S(1)} %bitcast.816), kind=kOutput, calls=%fused_computation.2 | convolution fusion | flops 549449728 | bytes 34635776 | tf_op jit(solution)/shard_map/qkgd,skd->kgqs/dot_general | solution.py:228
  433.1 8.3 %fusion.2 = bf16[4,2,512,1024]{2,3,1,0:T(8,128)(2,1)S(1)} fusion(f32[4,1024,512,2]{2,1,3,0:T(8,128)} %get-tuple-element.173, f32[4,2,512,1024]{2,3,1,0:T(8,128)S(1)} %bitcast.763, f32[4,2,512]{2,1,0:T(2,128)S(1)} %get-tuple-element.172, f32[4,2,512]{2,1,0:T(2,128)S(1)} %bitcast.859), kind=kLoop, calls=%fused_computation.4 | loop fusion | flops 16777216 | bytes 41975808 | tf_op jit(solution)/shard_map/convert_element_type | solution.py:232
  444.0 3.9 fusion.38
  457.5 4.0 fusion.42
  470.0 3.4 add_add_fusion.2
  483.2 5.4 collective-permute-done.12
  494.2 43.9 %all-reduce.8 = (f32[64]{0:T(128)}, f32[64]{0:T(128)}) all-reduce(f32[64]{0:T(128)S(1)} %get-tuple-element.120, f32[64]{0:T(128)S(1)} %get-tuple-element.122), channel_id=1, replica_groups=mesh['dp'=16,'tensor'=2] {'dp','tensor'}, use_global_device_ids=true, to_apply=%region_19.20 | all-reduce | flops 128 | bytes 1024 | tf_op jit(solution)/shard_map/psum | solution.py:273
  558.9 3.4 collective-permute-start.15
  581.0 3.4 collective-permute-done.7
  586.1 5.0 fusion.21
  591.1 38.6 %all-reduce.9 = (f32[1024]{0:T(1024)S(1)}, f32[1024]{0:T(1024)S(1)}) all-reduce(f32[1024]{0:T(1024)S(1)} %get-tuple-element.118, f32[1024]{0:T(1024)S(1)} %get-tuple-element.116), channel_id=2, replica_groups=mesh['dp'=16,'tensor'=2] {'dp'}, use_global_device_ids=true, to_apply=%region_17.18.clone | all-reduce | flops 2048 | bytes 16384
  630.9 7.3 %fusion.24 = bf16[1024,1024]{0,1:T(8,128)(2,1)} fusion(f32[1024,1024]{0,1:T(8,128)} %copy-done.9, bf16[1024,1024]{0,1:T(8,128)(2,1)S(1)} %copy-done.3, f32[1024]{0:T(1024)S(1)} %multiply_multiply_fusion.4, f32[1024]{0:T(1024)S(1)} %copy-done.84, f32[1024]{0:T(1024)S(1)} %copy-done.79, f32[1024,1024]{0,1:T(8,128)} %add_add_fusion.2, ...), kind=kLoop, calls=%fused_computation.47 | loop fusion | flops 9437184 | bytes 16789504 | tf_op jit(solution)/shard_map/convert_element_type | solution.py:272
  638.2 3.9 copy.89
  (450 shorter events, 220.3 us)
Async XLA Ops:
  51.8 17.0 %collective-permute-start = (f32[1024,1024]{0,1:T(8,128)}, f32[1024,1024]{0,1:T(8,128)}, u32[]{:S(2)}, u32[]{:S(2)}) collective-permute-start(f32[1024,1024]{0,1:T(8,128)} %fusion.58), channel_id=1, source_target_pairs={{0,1},{1,0},{2,3},{3,2},{4,5},{5,4},{6,7},{7,6},{8,9},{9,8},{10,11... | collective-permute-start | bytes 12582920 | tf_op jit(solution)/shard_map/ppermute | solution.py:66
  117.6 55.0 %collective-permute-start.48 = (f32[2,2,2,64,768]{4,3,2,1,0:T(8,128)}, f32[2,2,2,64,768]{4,3,2,1,0:T(8,128)}, u32[]{:S(2)}, u32[]{:S(2)}) collective-permute-start(f32[2,2,2,64,768]{4,3,2,1,0:T(8,128)} %dynamic-slice_bitcast_fusion.2), channel_id=1, source_target_pairs={{0,2},{2,0},{4,6},{6,4},{8,10},{10,8},{12,14},{14,12},{16,18},{18,... | collective-permute-start | bytes 4718600 | tf_op jit(solution)/shard_map/ppermute | solution.py:92
  121.4 51.7 %collective-permute-start.52 = (f32[2,2,2,64,768]{4,3,2,1,0:T(8,128)}, f32[2,2,2,64,768]{4,3,2,1,0:T(8,128)}, u32[]{:S(2)}, u32[]{:S(2)}) collective-permute-start(f32[2,2,2,64,768]{4,3,2,1,0:T(8,128)} %dynamic-slice_bitcast_fusion.1), channel_id=1, source_target_pairs={{0,4},{2,6},{4,0},{6,2},{8,12},{10,14},{12,8},{14,10},{16,20},{18,... | collective-permute-start | bytes 4718600 | tf_op jit(solution)/shard_map/ppermute | solution.py:92
  124.3 82.4 %collective-permute-start.56 = (f32[2,2,2,64,768]{4,3,2,1,0:T(8,128)}, f32[2,2,2,64,768]{4,3,2,1,0:T(8,128)}, u32[]{:S(2)}, u32[]{:S(2)}) collective-permute-start(f32[2,2,2,64,768]{4,3,2,1,0:T(8,128)} %dynamic-slice_bitcast_fusion), channel_id=1, source_target_pairs={{0,8},{2,10},{4,12},{6,14},{8,0},{10,2},{12,4},{14,6},{16,24},{18,... | collective-permute-start | bytes 4718600 | tf_op jit(solution)/shard_map/ppermute | solution.py:92
  139.4 50.0 %collective-permute-start.36 = (f32[2,2,2,64,768]{4,3,2,1,0:T(8,128)}, f32[2,2,2,64,768]{4,3,2,1,0:T(8,128)}, u32[]{:S(2)}, u32[]{:S(2)}) collective-permute-start(f32[2,2,2,64,768]{4,3,2,1,0:T(8,128)} %dynamic-slice_bitcast_fusion.5), channel_id=1, source_target_pairs={{0,2},{2,0},{4,6},{6,4},{8,10},{10,8},{12,14},{14,12},{16,18},{18,... | collective-permute-start | bytes 4718600 | tf_op jit(solution)/shard_map/ppermute | solution.py:92
  142.1 68.3 %collective-permute-start.40 = (f32[2,2,2,64,768]{4,3,2,1,0:T(8,128)}, f32[2,2,2,64,768]{4,3,2,1,0:T(8,128)S(1)}, u32[]{:S(2)}, u32[]{:S(2)}) collective-permute-start(f32[2,2,2,64,768]{4,3,2,1,0:T(8,128)} %dynamic-slice_bitcast_fusion.4), channel_id=1, source_target_pairs={{0,4},{2,6},{4,0},{6,2},{8,12},{10,14},{12,8},{14,10},{16,20},{18,... | collective-permute-start | bytes 4718600 | tf_op jit(solution)/shard_map/ppermute | solution.py:92
  172.6 38.3 %collective-permute-start.44 = (f32[2,2,2,64,768]{4,3,2,1,0:T(8,128)}, f32[2,2,2,64,768]{4,3,2,1,0:T(8,128)S(1)}, u32[]{:S(2)}, u32[]{:S(2)}) collective-permute-start(f32[2,2,2,64,768]{4,3,2,1,0:T(8,128)} %dynamic-slice_bitcast_fusion.3), channel_id=1, source_target_pairs={{0,8},{2,10},{4,12},{6,14},{8,0},{10,2},{12,4},{14,6},{16,24},{18,... | collective-permute-start | bytes 4718600 | tf_op jit(solution)/shard_map/ppermute | solution.py:92
  173.1 49.7 %collective-permute-start.24 = (f32[2,2,2,64,768]{4,3,2,1,0:T(8,128)}, f32[2,2,2,64,768]{4,3,2,1,0:T(8,128)S(1)}, u32[]{:S(2)}, u32[]{:S(2)}) collective-permute-start(f32[2,2,2,64,768]{4,3,2,1,0:T(8,128)} %dynamic-slice_bitcast_fusion.8), channel_id=1, source_target_pairs={{0,2},{2,0},{4,6},{6,4},{8,10},{10,8},{12,14},{14,12},{16,18},{18,... | collective-permute-start | bytes 4718600 | tf_op jit(solution)/shard_map/ppermute | solution.py:92
  189.4 37.5 %collective-permute-start.28 = (f32[2,2,2,64,768]{4,3,2,1,0:T(8,128)}, f32[2,2,2,64,768]{4,3,2,1,0:T(8,128)S(1)}, u32[]{:S(2)}, u32[]{:S(2)}) collective-permute-start(f32[2,2,2,64,768]{4,3,2,1,0:T(8,128)} %dynamic-slice_bitcast_fusion.7), channel_id=1, source_target_pairs={{0,4},{2,6},{4,0},{6,2},{8,12},{10,14},{12,8},{14,10},{16,20},{18,... | collective-permute-start | bytes 4718600 | tf_op jit(solution)/shard_map/ppermute | solution.py:92
  206.6 37.6 %collective-permute-start.32 = (f32[2,2,2,64,768]{4,3,2,1,0:T(8,128)}, f32[2,2,2,64,768]{4,3,2,1,0:T(8,128)}, u32[]{:S(2)}, u32[]{:S(2)}) collective-permute-start(f32[2,2,2,64,768]{4,3,2,1,0:T(8,128)} %dynamic-slice_bitcast_fusion.6), channel_id=1, source_target_pairs={{0,8},{2,10},{4,12},{6,14},{8,0},{10,2},{12,4},{14,6},{16,24},{18,... | collective-permute-start | bytes 4718600 | tf_op jit(solution)/shard_map/ppermute | solution.py:92
  210.3 35.6 %collective-permute-start.49 = (f32[2,2,64,768]{3,2,1,0:T(8,128)}, f32[2,2,64,768]{3,2,1,0:T(8,128)}, u32[]{:S(2)}, u32[]{:S(2)}) collective-permute-start(f32[2,2,64,768]{3,2,1,0:T(8,128)} %bitcast_add_fusion.2), channel_id=1, source_target_pairs={{0,4},{2,6},{4,0},{6,2},{8,12},{10,14},{12,8},{14,10},{16,20},{18,... | collective-permute-start | bytes 2359304 | tf_op jit(solution)/shard_map/ppermute | solution.py:92
  210.9 50.2 %collective-permute-start.53 = (f32[2,2,64,768]{3,2,1,0:T(8,128)}, f32[2,2,64,768]{3,2,1,0:T(8,128)}, u32[]{:S(2)}, u32[]{:S(2)}) collective-permute-start(f32[2,2,64,768]{3,2,1,0:T(8,128)} %bitcast_add_fusion.1), channel_id=1, source_target_pairs={{0,8},{2,10},{4,12},{6,14},{8,0},{10,2},{12,4},{14,6},{16,24},{18,... | collective-permute-start | bytes 2359304 | tf_op jit(solution)/shard_map/ppermute | solution.py:92
  222.8 39.6 %collective-permute-start.57 = (f32[2,2,64,768]{3,2,1,0:T(8,128)}, f32[2,2,64,768]{3,2,1,0:T(8,128)}, u32[]{:S(2)}, u32[]{:S(2)}) collective-permute-start(f32[2,2,64,768]{3,2,1,0:T(8,128)} %bitcast_add_fusion), channel_id=1, source_target_pairs={{0,2},{2,0},{4,6},{6,4},{8,10},{10,8},{12,14},{14,12},{16,18},{18,... | collective-permute-start | bytes 2359304 | tf_op jit(solution)/shard_map/ppermute | solution.py:92
  226.9 38.9 %collective-permute-start.37 = (f32[2,2,64,768]{3,2,1,0:T(8,128)}, f32[2,2,64,768]{3,2,1,0:T(8,128)S(1)}, u32[]{:S(2)}, u32[]{:S(2)}) collective-permute-start(f32[2,2,64,768]{3,2,1,0:T(8,128)} %bitcast_add_fusion.5), channel_id=1, source_target_pairs={{0,4},{2,6},{4,0},{6,2},{8,12},{10,14},{12,8},{14,10},{16,20},{18,... | collective-permute-start | bytes 2359304 | tf_op jit(solution)/shard_map/ppermute | solution.py:92
  244.3 33.6 %collective-permute-start.41 = (f32[2,2,64,768]{3,2,1,0:T(8,128)S(1)}, f32[2,2,64,768]{3,2,1,0:T(8,128)S(1)}, u32[]{:S(2)}, u32[]{:S(2)}) collective-permute-start(f32[2,2,64,768]{3,2,1,0:T(8,128)S(1)} %bitcast_add_fusion.4), channel_id=1, source_target_pairs={{0,8},{2,10},{4,12},{6,14},{8,0},{10,2},{12,4},{14,6},{16,24},{18,... | collective-permute-start | bytes 2359304 | tf_op jit(solution)/shard_map/ppermute | solution.py:92
  246.0 33.6 %collective-permute-start.45 = (f32[2,2,64,768]{3,2,1,0:T(8,128)S(1)}, f32[2,2,64,768]{3,2,1,0:T(8,128)S(1)}, u32[]{:S(2)}, u32[]{:S(2)}) collective-permute-start(f32[2,2,64,768]{3,2,1,0:T(8,128)S(1)} %bitcast_add_fusion.3), channel_id=1, source_target_pairs={{0,2},{2,0},{4,6},{6,4},{8,10},{10,8},{12,14},{14,12},{16,18},{18,... | collective-permute-start | bytes 2359304 | tf_op jit(solution)/shard_map/ppermute | solution.py:92
  261.1 20.1 %collective-permute-start.25 = (f32[2,2,64,768]{3,2,1,0:T(8,128)S(1)}, f32[2,2,64,768]{3,2,1,0:T(8,128)S(1)}, u32[]{:S(2)}, u32[]{:S(2)}) collective-permute-start(f32[2,2,64,768]{3,2,1,0:T(8,128)S(1)} %bitcast_add_fusion.8), channel_id=1, source_target_pairs={{0,4},{2,6},{4,0},{6,2},{8,12},{10,14},{12,8},{14,10},{16,20},{18,... | collective-permute-start | bytes 2359304 | tf_op jit(solution)/shard_map/ppermute | solution.py:92
  262.5 32.3 %collective-permute-start.29 = (f32[2,2,64,768]{3,2,1,0:T(8,128)S(1)}, f32[2,2,64,768]{3,2,1,0:T(8,128)S(1)}, u32[]{:S(2)}, u32[]{:S(2)}) collective-permute-start(f32[2,2,64,768]{3,2,1,0:T(8,128)S(1)} %bitcast_add_fusion.7), channel_id=1, source_target_pairs={{0,8},{2,10},{4,12},{6,14},{8,0},{10,2},{12,4},{14,6},{16,24},{18,... | collective-permute-start | bytes 2359304 | tf_op jit(solution)/shard_map/ppermute | solution.py:92
  265.9 29.0 %collective-permute-start.33 = (f32[2,2,64,768]{3,2,1,0:T(8,128)S(1)}, f32[2,2,64,768]{3,2,1,0:T(8,128)S(1)}, u32[]{:S(2)}, u32[]{:S(2)}) collective-permute-start(f32[2,2,64,768]{3,2,1,0:T(8,128)S(1)} %bitcast_add_fusion.6), channel_id=1, source_target_pairs={{0,2},{2,0},{4,6},{6,4},{8,10},{10,8},{12,14},{14,12},{16,18},{18,... | collective-permute-start | bytes 2359304 | tf_op jit(solution)/shard_map/ppermute | solution.py:92
  277.9 25.3 %collective-permute-start.50 = (f32[2,64,768]{2,1,0:T(8,128)S(1)}, f32[2,64,768]{2,1,0:T(8,128)S(1)}, u32[]{:S(2)}, u32[]{:S(2)}) collective-permute-start(f32[2,64,768]{2,1,0:T(8,128)S(1)} %bitcast_add_fusion.13), channel_id=1, source_target_pairs={{0,8},{2,10},{4,12},{6,14},{8,0},{10,2},{12,4},{14,6},{16,24},{18,... | collective-permute-start | bytes 1179656 | tf_op jit(solution)/shard_map/ppermute | solution.py:92
  279.6 25.1 %collective-permute-start.54 = (f32[2,64,768]{2,1,0:T(8,128)S(1)}, f32[2,64,768]{2,1,0:T(8,128)S(1)}, u32[]{:S(2)}, u32[]{:S(2)}) collective-permute-start(f32[2,64,768]{2,1,0:T(8,128)S(1)} %bitcast_add_fusion.11), channel_id=1, source_target_pairs={{0,2},{2,0},{4,6},{6,4},{8,10},{10,8},{12,14},{14,12},{16,18},{18,... | collective-permute-start | bytes 1179656 | tf_op jit(solution)/shard_map/ppermute | solution.py:92
  281.2 118.7 %collective-permute-start.2 = (f32[1024,1024]{0,1:T(8,128)S(1)}, f32[1024,1024]{0,1:T(8,128)S(1)}, u32[]{:S(2)}, u32[]{:S(2)}) collective-permute-start(f32[1024,1024]{0,1:T(8,128)S(1)} %convolution_add_fusion), channel_id=1, source_target_pairs={{0,1},{1,0},{2,3},{3,2},{4,5},{5,4},{6,7},{7,6},{8,9},{9,8},{10,11... | collective-permute-start | bytes 12582920 | tf_op jit(solution)/shard_map/ppermute | solution.py:66
  294.7 12.8 %collective-permute-start.58 = (f32[2,64,768]{2,1,0:T(8,128)S(1)}, f32[2,64,768]{2,1,0:T(8,128)S(1)}, u32[]{:S(2)}, u32[]{:S(2)}) collective-permute-start(f32[2,64,768]{2,1,0:T(8,128)S(1)} %bitcast_add_fusion.9), channel_id=1, source_target_pairs={{0,4},{2,6},{4,0},{6,2},{8,12},{10,14},{12,8},{14,10},{16,20},{18,... | collective-permute-start | bytes 1179656 | tf_op jit(solution)/shard_map/ppermute | solution.py:92
  294.9 16.7 %collective-permute-start.38 = (f32[2,64,768]{2,1,0:T(8,128)S(1)}, f32[2,64,768]{2,1,0:T(8,128)S(1)}, u32[]{:S(2)}, u32[]{:S(2)}) collective-permute-start(f32[2,64,768]{2,1,0:T(8,128)S(1)} %bitcast_add_fusion.19), channel_id=1, source_target_pairs={{0,8},{2,10},{4,12},{6,14},{8,0},{10,2},{12,4},{14,6},{16,24},{18,... | collective-permute-start | bytes 1179656 | tf_op jit(solution)/shard_map/ppermute | solution.py:92
  303.2 10.9 %collective-permute-start.42 = (f32[2,64,768]{2,1,0:T(8,128)S(1)}, f32[2,64,768]{2,1,0:T(8,128)S(1)}, u32[]{:S(2)}, u32[]{:S(2)}) collective-permute-start(f32[2,64,768]{2,1,0:T(8,128)S(1)} %bitcast_add_fusion.17), channel_id=1, source_target_pairs={{0,2},{2,0},{4,6},{6,4},{8,10},{10,8},{12,14},{14,12},{16,18},{18,... | collective-permute-start | bytes 1179656 | tf_op jit(solution)/shard_map/ppermute | solution.py:92
  307.5 11.1 %collective-permute-start.26 = (f32[2,64,768]{2,1,0:T(8,128)S(1)}, f32[2,64,768]{2,1,0:T(8,128)S(1)}, u32[]{:S(2)}, u32[]{:S(2)}) collective-permute-start(f32[2,64,768]{2,1,0:T(8,128)S(1)} %bitcast_add_fusion.25), channel_id=1, source_target_pairs={{0,8},{2,10},{4,12},{6,14},{8,0},{10,2},{12,4},{14,6},{16,24},{18,... | collective-permute-start | bytes 1179656 | tf_op jit(solution)/shard_map/ppermute | solution.py:92
  314.1 87.4 %collective-permute-start.1 = (f32[1024,1024]{0,1:T(8,128)}, f32[1024,1024]{0,1:T(8,128)}, u32[]{:S(2)}, u32[]{:S(2)}) collective-permute-start(f32[1024,1024]{0,1:T(8,128)} %fusion.93), channel_id=1, source_target_pairs={{0,1},{1,0},{2,3},{3,2},{4,5},{5,4},{6,7},{7,6},{8,9},{9,8},{10,11... | collective-permute-start | bytes 12582920 | tf_op jit(solution)/shard_map/ppermute | solution.py:66
  314.2 11.5 %collective-permute-start.34 = (f32[2,64,768]{2,1,0:T(8,128)S(1)}, f32[2,64,768]{2,1,0:T(8,128)S(1)}, u32[]{:S(2)}, u32[]{:S(2)}) collective-permute-start(f32[2,64,768]{2,1,0:T(8,128)S(1)} %bitcast_add_fusion.21), channel_id=1, source_target_pairs={{0,4},{2,6},{4,0},{6,2},{8,12},{10,14},{12,8},{14,10},{16,20},{18,... | collective-permute-start | bytes 1179656 | tf_op jit(solution)/shard_map/ppermute | solution.py:92
  318.6 19.2 %collective-permute-start.51 = (f32[64,768]{1,0:T(8,128)S(1)}, f32[64,768]{1,0:T(8,128)S(1)}, u32[]{:S(2)}, u32[]{:S(2)}) collective-permute-start(f32[64,768]{1,0:T(8,128)S(1)} %bitcast_add_fusion.45), channel_id=1, source_target_pairs={{0,16},{2,18},{4,20},{6,22},{8,24},{10,26},{12,28},{14,30},{16,0},... | collective-permute-start | bytes 589832 | tf_op jit(solution)/shard_map/ppermute | solution.py:92
  322.2 24.1 %collective-permute-start.55 = (f32[64,768]{1,0:T(8,128)S(1)}, f32[64,768]{1,0:T(8,128)S(1)}, u32[]{:S(2)}, u32[]{:S(2)}) collective-permute-start(f32[64,768]{1,0:T(8,128)S(1)} %bitcast_add_fusion.39), channel_id=1, source_target_pairs={{0,16},{2,18},{4,20},{6,22},{8,24},{10,26},{12,28},{14,30},{16,0},... | collective-permute-start | bytes 589832 | tf_op jit(solution)/shard_map/ppermute | solution.py:92
  325.7 29.0 %collective-permute-start.59 = (f32[64,768]{1,0:T(8,128)S(1)}, f32[64,768]{1,0:T(8,128)S(1)}, u32[]{:S(2)}, u32[]{:S(2)}) collective-permute-start(f32[64,768]{1,0:T(8,128)S(1)} %bitcast_add_fusion.33), channel_id=1, source_target_pairs={{0,16},{2,18},{4,20},{6,22},{8,24},{10,26},{12,28},{14,30},{16,0},... | collective-permute-start | bytes 589832 | tf_op jit(solution)/shard_map/ppermute | solution.py:92
  337.8 25.3 %collective-permute-start.39 = (f32[64,768]{1,0:T(8,128)S(1)}, f32[64,768]{1,0:T(8,128)S(1)}, u32[]{:S(2)}, u32[]{:S(2)}) collective-permute-start(f32[64,768]{1,0:T(8,128)S(1)} %bitcast_add_fusion.63), channel_id=1, source_target_pairs={{0,16},{2,18},{4,20},{6,22},{8,24},{10,26},{12,28},{14,30},{16,0},... | collective-permute-start | bytes 589832 | tf_op jit(solution)/shard_map/ppermute | solution.py:92
  346.3 25.3 %collective-permute-start.43 = (f32[64,768]{1,0:T(8,128)S(1)}, f32[64,768]{1,0:T(8,128)S(1)}, u32[]{:S(2)}, u32[]{:S(2)}) collective-permute-start(f32[64,768]{1,0:T(8,128)S(1)} %bitcast_add_fusion.57), channel_id=1, source_target_pairs={{0,16},{2,18},{4,20},{6,22},{8,24},{10,26},{12,28},{14,30},{16,0},... | collective-permute-start | bytes 589832 | tf_op jit(solution)/shard_map/ppermute | solution.py:92
  354.7 25.3 %collective-permute-start.47 = (f32[64,768]{1,0:T(8,128)S(1)}, f32[64,768]{1,0:T(8,128)S(1)}, u32[]{:S(2)}, u32[]{:S(2)}) collective-permute-start(f32[64,768]{1,0:T(8,128)S(1)} %bitcast_add_fusion.51), channel_id=1, source_target_pairs={{0,16},{2,18},{4,20},{6,22},{8,24},{10,26},{12,28},{14,30},{16,0},... | collective-permute-start | bytes 589832 | tf_op jit(solution)/shard_map/ppermute | solution.py:92
  363.1 25.3 %collective-permute-start.27 = (f32[64,768]{1,0:T(8,128)S(1)}, f32[64,768]{1,0:T(8,128)S(1)}, u32[]{:S(2)}, u32[]{:S(2)}) collective-permute-start(f32[64,768]{1,0:T(8,128)S(1)} %bitcast_add_fusion.81), channel_id=1, source_target_pairs={{0,16},{2,18},{4,20},{6,22},{8,24},{10,26},{12,28},{14,30},{16,0},... | collective-permute-start | bytes 589832 | tf_op jit(solution)/shard_map/ppermute | solution.py:92
  371.5 21.1 %collective-permute-start.31 = (f32[64,768]{1,0:T(8,128)S(1)}, f32[64,768]{1,0:T(8,128)S(1)}, u32[]{:S(2)}, u32[]{:S(2)}) collective-permute-start(f32[64,768]{1,0:T(8,128)S(1)} %bitcast_add_fusion.75), channel_id=1, source_target_pairs={{0,16},{2,18},{4,20},{6,22},{8,24},{10,26},{12,28},{14,30},{16,0},... | collective-permute-start | bytes 589832 | tf_op jit(solution)/shard_map/ppermute | solution.py:92
  380.0 16.5 %collective-permute-start.35 = (f32[64,768]{1,0:T(8,128)S(1)}, f32[64,768]{1,0:T(8,128)S(1)}, u32[]{:S(2)}, u32[]{:S(2)}) collective-permute-start(f32[64,768]{1,0:T(8,128)S(1)} %bitcast_add_fusion.69), channel_id=1, source_target_pairs={{0,16},{2,18},{4,20},{6,22},{8,24},{10,26},{12,28},{14,30},{16,0},... | collective-permute-start | bytes 589832 | tf_op jit(solution)/shard_map/ppermute | solution.py:92
  455.6 22.5 %collective-permute-start.16 = (f32[2,2,2,64,256]{4,3,2,1,0:T(8,128)}, f32[2,2,2,64,256]{4,3,2,1,0:T(8,128)}, u32[]{:S(2)}, u32[]{:S(2)}) collective-permute-start(f32[2,2,2,64,256]{4,3,2,1,0:T(8,128)} %dynamic-slice_bitcast_fusion.12), channel_id=1, source_target_pairs={{0,2},{2,0},{4,6},{6,4},{8,10},{10,8},{12,14},{14,12},{16,18},{18,... | collective-permute-start | bytes 1572872 | tf_op jit(solution)/shard_map/ppermute | solution.py:92
  456.9 25.1 %collective-permute-start.20 = (f32[2,2,2,64,256]{4,3,2,1,0:T(8,128)}, f32[2,2,2,64,256]{4,3,2,1,0:T(8,128)}, u32[]{:S(2)}, u32[]{:S(2)}) collective-permute-start(f32[2,2,2,64,256]{4,3,2,1,0:T(8,128)} %dynamic-slice_bitcast_fusion.11), channel_id=1, source_target_pairs={{0,4},{2,6},{4,0},{6,2},{8,12},{10,14},{12,8},{14,10},{16,20},{18,... | collective-permute-start | bytes 1572872 | tf_op jit(solution)/shard_map/ppermute | solution.py:92
  473.4 112.7 %collective-permute-start.3 = (f32[1024,1024]{0,1:T(8,128)}, f32[1024,1024]{0,1:T(8,128)}, u32[]{:S(2)}, u32[]{:S(2)}) collective-permute-start(f32[1024,1024]{0,1:T(8,128)} %add_add_fusion.2), channel_id=1, source_target_pairs={{0,1},{1,0},{2,3},{3,2},{4,5},{5,4},{6,7},{7,6},{8,9},{9,8},{10,11... | collective-permute-start | bytes 12582920 | tf_op jit(solution)/shard_map/ppermute | solution.py:66
  474.2 14.4 %collective-permute-start.12 = (f32[2,2,2,64,256]{4,3,2,1,0:T(8,128)S(1)}, f32[2,2,2,64,256]{4,3,2,1,0:T(8,128)S(1)}, u32[]{:S(2)}, u32[]{:S(2)}) collective-permute-start(f32[2,2,2,64,256]{4,3,2,1,0:T(8,128)S(1)} %dynamic-slice_bitcast_fusion.13), channel_id=1, source_target_pairs={{0,8},{2,10},{4,12},{6,14},{8,0},{10,2},{12,4},{14,6},{16,24},{18,... | collective-permute-start | bytes 1572872 | tf_op jit(solution)/shard_map/ppermute | solution.py:92
  477.2 68.2 %collective-permute-start.4 = (f32[2,2,2,64,384]{4,3,2,1,0:T(8,128)}, f32[2,2,2,64,384]{4,3,2,1,0:T(8,128)}, u32[]{:S(2)}, u32[]{:S(2)}) collective-permute-start(f32[2,2,2,64,384]{4,3,2,1,0:T(8,128)} %dynamic-slice_bitcast_fusion.10), channel_id=1, source_target_pairs={{0,2},{2,0},{4,6},{6,4},{8,10},{10,8},{12,14},{14,12},{16,18},{18,... | collective-permute-start | bytes 2359304 | tf_op jit(solution)/shard_map/ppermute | solution.py:92
  479.1 10.9 %collective-permute-start.17 = (f32[2,2,64,256]{3,2,1,0:T(8,128)S(1)}, f32[2,2,64,256]{3,2,1,0:T(8,128)S(1)}, u32[]{:S(2)}, u32[]{:S(2)}) collective-permute-start(f32[2,2,64,256]{3,2,1,0:T(8,128)S(1)} %bitcast_add_fusion.30), channel_id=1, source_target_pairs={{0,4},{2,6},{4,0},{6,2},{8,12},{10,14},{12,8},{14,10},{16,20},{18,... | collective-permute-start | bytes 786440 | tf_op jit(solution)/shard_map/ppermute | solution.py:92
  482.1 65.3 %collective-permute-start.8 = (f32[2,2,2,64,384]{4,3,2,1,0:T(8,128)}, f32[2,2,2,64,384]{4,3,2,1,0:T(8,128)}, u32[]{:S(2)}, u32[]{:S(2)}) collective-permute-start(f32[2,2,2,64,384]{4,3,2,1,0:T(8,128)} %dynamic-slice_bitcast_fusion.9), channel_id=1, source_target_pairs={{0,4},{2,6},{4,0},{6,2},{8,12},{10,14},{12,8},{14,10},{16,20},{18,... | collective-permute-start | bytes 2359304 | tf_op jit(solution)/shard_map/ppermute | solution.py:92
  488.6 50.5 %collective-permute-start.21 = (f32[2,2,64,256]{3,2,1,0:T(8,128)S(1)}, f32[2,2,64,256]{3,2,1,0:T(8,128)}, u32[]{:S(2)}, u32[]{:S(2)}) collective-permute-start(f32[2,2,64,256]{3,2,1,0:T(8,128)S(1)} %bitcast_add_fusion.29), channel_id=1, source_target_pairs={{0,8},{2,10},{4,12},{6,14},{8,0},{10,2},{12,4},{14,6},{16,24},{18,... | collective-permute-start | bytes 786440 | tf_op jit(solution)/shard_map/ppermute | solution.py:92
  490.0 52.0 %collective-permute-start.13 = (f32[2,2,64,256]{3,2,1,0:T(8,128)}, f32[2,2,64,256]{3,2,1,0:T(8,128)}, u32[]{:S(2)}, u32[]{:S(2)}) collective-permute-start(f32[2,2,64,256]{3,2,1,0:T(8,128)} %bitcast_add_fusion.31), channel_id=1, source_target_pairs={{0,2},{2,0},{4,6},{6,4},{8,10},{10,8},{12,14},{14,12},{16,18},{18,... | collective-permute-start | bytes 786440 | tf_op jit(solution)/shard_map/ppermute | solution.py:92
  547.3 20.6 %collective-permute-start.5 = (f32[2,2,64,384]{3,2,1,0:T(8,128)S(1)}, f32[2,2,64,384]{3,2,1,0:T(8,128)S(1)}, u32[]{:S(2)}, u32[]{:S(2)}) collective-permute-start(f32[2,2,64,384]{3,2,1,0:T(8,128)S(1)} %bitcast_add_fusion.28), channel_id=1, source_target_pairs={{0,4},{2,6},{4,0},{6,2},{8,12},{10,14},{12,8},{14,10},{16,20},{18,... | collective-permute-start | bytes 1179656 | tf_op jit(solution)/shard_map/ppermute | solution.py:92
  550.0 16.1 %collective-permute-start.9 = (f32[2,2,64,384]{3,2,1,0:T(8,128)S(1)}, f32[2,2,64,384]{3,2,1,0:T(8,128)S(1)}, u32[]{:S(2)}, u32[]{:S(2)}) collective-permute-start(f32[2,2,64,384]{3,2,1,0:T(8,128)S(1)} %bitcast_add_fusion.27), channel_id=1, source_target_pairs={{0,8},{2,10},{4,12},{6,14},{8,0},{10,2},{12,4},{14,6},{16,24},{18,... | collective-permute-start | bytes 1179656 | tf_op jit(solution)/shard_map/ppermute | solution.py:92
  (114 other events, 1080.1 us)
